TPU v7x, 256 devices: a whole 4x4x8 slice. The times are simulated.
256 devices in a mesh: row: 64 (over y, z, core), col: 4 (over x).
Axes of the slice: x: 4, y: 4, z: 8, core: 2. Of those that a mesh axis runs over, the one named last changes fastest.
Arguments:
- factor: float32 [16384, 64, 256], P('row', 'col'), may hold values from -0.046875 to 0.046875
- diag_inverse: float32 [16384, 2048], P('row'), as said below
- phenotypes: float32 [16384, 512], P('row', 'col'), may hold values from -6 to 6
Outputs:
- solution: float32 [16384, 512], P('row', 'col')
Inputs may be any that keep to these rules, and one draw needn't show every extreme that they name: `diag_inverse`: each 2048 x 2048 panel inverse is lower triangular with a diagonal between 0.5 and 1.5.
All inputs are finite; a program needn't handle non-finite values.
Results may differ from a plain program's by a relative error of at most 0.0001.
Values sent between devices are 32-bit elements; how exact they have to be, the bound alone decides.
No kernel may reach another device: no remote copies, remote signals or barrier semaphores. Data moves between devices by JAX's collectives and lax.ppermute only.
A program may use at most 128 MiB of HBM per device.

v0:
```python
import jax
import jax.numpy as jnp
from jax import lax
from jax.sharding import PartitionSpec as P


def shards(factor, diag_inverse, phenotypes):
    my_row = lax.axis_index("row")
    rows_here = phenotypes.shape[0]
    panel_rows = diag_inverse.shape[1]
    per_panel = panel_rows // rows_here
    my_panel = my_row // per_panel
    my_offset = my_row % per_panel * rows_here
    local_blocks = factor.shape[1]
    panel_count = local_blocks * lax.axis_size("col") // per_panel
    whole_factor = lax.all_gather(factor, "col", axis=1, tiled=True)
    flat_factor = whole_factor.reshape(rows_here, -1)
    empty = jnp.zeros(phenotypes.shape, jnp.float32)

    def solve_mine(residual):
        return lax.dot_general(
            diag_inverse,
            residual,
            (((0,), (0,)), ((), ())),
            precision=lax.Precision.HIGHEST,
            preferred_element_type=jnp.float32,
        )

    def solve_none(residual):
        return jnp.zeros((panel_rows, residual.shape[1]), jnp.float32)

    def advance(panel_index, carry):
        running, solved = carry
        columns = lax.dynamic_slice_in_dim(flat_factor, panel_index * panel_rows, panel_rows, 1)
        residual = phenotypes - running
        term = lax.cond(my_panel == panel_index, solve_mine, solve_none, residual)
        panel_solved = lax.psum(term, "row")
        mine = lax.dynamic_slice_in_dim(panel_solved, my_offset, rows_here, 0)
        solved = jnp.where(my_panel == panel_index, mine, solved)
        running = running + jnp.dot(
            columns,
            panel_solved,
            precision=lax.Precision.HIGHEST,
            preferred_element_type=jnp.float32,
        )
        return (running, solved)

    running, solution = lax.fori_loop(0, panel_count, advance, (empty, empty))
    return solution


def solution(mesh):
    placed = (P("row", "col", None), P("row", None), P("row", "col"))
    return jax.shard_map(
        shards, mesh=mesh, in_specs=placed, out_specs=P("row", "col"), check_vma=False
    )
```

profile of v0, /device:TPU:2, one launch (start us, length us, event | category | flops | bytes accessed | tf_op | source)
XLA Modules:
  0.0 1734.9 jit_solution(15123583881384055721)
XLA Ops:
  6.5 0.7 all-gather.2.cloned.1.call-update
  7.3 161.4 %all-gather.2.cloned.1.call-done = f32[256,64,256]{2,1,0:T(8,128)} async-done(((f32[256,16,256]{2,1,0:T(8,128)}), f32[256,64,256]{2,1,0:T(8,128)}) %all-gather.2.cloned.1.call-update) | async-done | bytes 16777232 | tf_op jit(solution)/shard_map/all_gather | solution.py:16
  168.7 18.6 %copy.5 = f32[32,8,64,256]{3,1,2,0:T(8,128)} copy(f32[32,8,64,256]{3,2,1,0:T(8,128)} %bitcast.9) | data formatting | bytes 33554432
  187.3 1540.3 %while.18 = (s32[]{:T(128)}, f32[256,128]{1,0:T(8,128)S(1)}, f32[256,128]{0,1:T(8,128)S(1)}, f32[256,16384]{1,0:T(8,128)}, s32[]{:T(128)}, /*index=5*/f32[256,12...) while((s32[]{:T(128)}, f32[256,128]{1,0:T(8,128)S(1)}, ...), condition=%wide.region_4.5_spmd.clone, body=%wide.region_0.4_spmd.clone.sunk | while | flops 1611038720 | bytes 17957160 | solution.py:48
  187.3 2.2 conditional.3
  187.4 2.1 convolution_bitcast_fusion
  189.5 1.0 copy-done
  190.5 0.0 all-reduce.2.cloned.1.call-update
  190.6 187.4 %all-reduce.2.cloned.1.call-done = f32[2048,128]{0,1:T(8,128)} async-done(((f32[2048,128]{0,1:T(8,128)}), f32[2048,128]{0,1:T(8,128)}) %all-reduce.2.cloned.1.call-update) | async-done | bytes 1048592 | tf_op jit(solution)/shard_map/while/body/eval_jaxpr/psum | solution.py:37
  378.0 3.7 fusion.14
  381.7 0.9 select_select_fusion.2
  382.6 0.0 all-reduce.2.cloned.1.call-start
  382.7 0.1 conditional.3
  382.7 0.1 broadcast.4
  382.8 1.0 copy-done
  383.9 0.0 all-reduce.2.cloned.1.call-update
  383.9 186.4 %all-reduce.2.cloned.1.call-done = f32[2048,128]{0,1:T(8,128)} async-done(((f32[2048,128]{0,1:T(8,128)}), f32[2048,128]{0,1:T(8,128)}) %all-reduce.2.cloned.1.call-update) | async-done | bytes 1048592 | tf_op jit(solution)/shard_map/while/body/eval_jaxpr/psum | solution.py:37
  570.3 3.7 fusion.14
  574.0 0.9 select_select_fusion.2
  575.0 0.0 all-reduce.2.cloned.1.call-start
  575.0 0.1 conditional.3
  575.1 0.1 broadcast.4
  575.2 1.0 copy-done
  576.2 0.0 all-reduce.2.cloned.1.call-update
  576.2 186.1 %all-reduce.2.cloned.1.call-done = f32[2048,128]{0,1:T(8,128)} async-done(((f32[2048,128]{0,1:T(8,128)}), f32[2048,128]{0,1:T(8,128)}) %all-reduce.2.cloned.1.call-update) | async-done | bytes 1048592 | tf_op jit(solution)/shard_map/while/body/eval_jaxpr/psum | solution.py:37
  762.4 3.7 fusion.14
  766.0 0.9 select_select_fusion.2
  767.0 0.0 all-reduce.2.cloned.1.call-start
  767.1 0.1 conditional.3
  767.1 0.1 broadcast.4
  767.2 1.0 copy-done
  768.2 0.0 all-reduce.2.cloned.1.call-update
  768.3 185.6 %all-reduce.2.cloned.1.call-done = f32[2048,128]{0,1:T(8,128)} async-done(((f32[2048,128]{0,1:T(8,128)}), f32[2048,128]{0,1:T(8,128)}) %all-reduce.2.cloned.1.call-update) | async-done | bytes 1048592 | tf_op jit(solution)/shard_map/while/body/eval_jaxpr/psum | solution.py:37
  953.9 3.7 fusion.14
  957.5 0.9 select_select_fusion.2
  958.5 0.0 all-reduce.2.cloned.1.call-start
  958.6 0.1 conditional.3
  958.6 0.1 broadcast.4
  958.7 1.0 copy-done
  959.7 186.1 %all-reduce.2.cloned.1.call-done = f32[2048,128]{0,1:T(8,128)} async-done(((f32[2048,128]{0,1:T(8,128)}), f32[2048,128]{0,1:T(8,128)}) %all-reduce.2.cloned.1.call-update) | async-done | bytes 1048592 | tf_op jit(solution)/shard_map/while/body/eval_jaxpr/psum | solution.py:37
  1145.9 3.7 fusion.14
  1149.6 0.9 select_select_fusion.2
  1150.5 0.0 all-reduce.2.cloned.1.call-start
  1150.6 0.1 conditional.3
  1150.6 0.1 broadcast.4
  1150.7 1.0 copy-done
  1151.8 186.5 %all-reduce.2.cloned.1.call-done = f32[2048,128]{0,1:T(8,128)} async-done(((f32[2048,128]{0,1:T(8,128)}), f32[2048,128]{0,1:T(8,128)}) %all-reduce.2.cloned.1.call-update) | async-done | bytes 1048592 | tf_op jit(solution)/shard_map/while/body/eval_jaxpr/psum | solution.py:37
  1338.2 3.7 fusion.14
  1341.9 0.9 select_select_fusion.2
  1342.9 0.0 all-reduce.2.cloned.1.call-start
  1343.0 0.1 conditional.3
  1343.0 0.1 broadcast.4
  1343.1 1.0 copy-done
  1344.1 186.5 %all-reduce.2.cloned.1.call-done = f32[2048,128]{0,1:T(8,128)} async-done(((f32[2048,128]{0,1:T(8,128)}), f32[2048,128]{0,1:T(8,128)}) %all-reduce.2.cloned.1.call-update) | async-done | bytes 1048592 | tf_op jit(solution)/shard_map/while/body/eval_jaxpr/psum | solution.py:37
  1530.6 3.7 fusion.14
  1534.3 0.9 select_select_fusion.2
  1535.2 0.0 all-reduce.2.cloned.1.call-start
  1535.3 0.1 conditional.3
  1535.3 0.1 broadcast.4
  1535.5 1.0 copy-done
  1536.5 186.4 %all-reduce.2.cloned.1.call-done = f32[2048,128]{0,1:T(8,128)} async-done(((f32[2048,128]{0,1:T(8,128)}), f32[2048,128]{0,1:T(8,128)}) %all-reduce.2.cloned.1.call-update) | async-done | bytes 1048592 | tf_op jit(solution)/shard_map/while/body/eval_jaxpr/psum | solution.py:37
  1722.9 3.7 fusion.14
  1726.6 0.9 select_select_fusion.2
  1727.6 0.8 copy.4
  (26 shorter events, 0.2 us)
Async XLA Ops:
  6.5 162.2 %all-gather.2.cloned.1.call-start = ((), (), s32[]{:S(2)}) async-start(), calls=%async_computation | async-start | bytes 20971520 | tf_op jit(solution)/shard_map/all_gather | solution.py:16
  168.7 18.6 %copy-start.1 = (f32[256,2048]{1,0:T(8,128)S(1)}, f32[256,2048]{1,0:T(8,128)}, u32[]{:S(2)}) copy-start(f32[256,2048]{1,0:T(8,128)} %param.8) | copy-start | bytes 6291460
  187.3 190.7 %all-reduce.2.cloned.1.call-start = ((), (), s32[]{:S(2)}) async-start(), calls=%async_computation.1 | async-start | bytes 2097152 | tf_op jit(solution)/shard_map/while/body/eval_jaxpr/psum | solution.py:37
  189.5 1.0 copy-start
  382.6 187.7 %all-reduce.2.cloned.1.call-start = ((), (), s32[]{:S(2)}) async-start(), calls=%async_computation.1 | async-start | bytes 2097152 | tf_op jit(solution)/shard_map/while/body/eval_jaxpr/psum | solution.py:37
  382.8 1.0 copy-start
  575.0 187.4 %all-reduce.2.cloned.1.call-start = ((), (), s32[]{:S(2)}) async-start(), calls=%async_computation.1 | async-start | bytes 2097152 | tf_op jit(solution)/shard_map/while/body/eval_jaxpr/psum | solution.py:37
  575.2 1.0 copy-start
  767.0 186.8 %all-reduce.2.cloned.1.call-start = ((), (), s32[]{:S(2)}) async-start(), calls=%async_computation.1 | async-start | bytes 2097152 | tf_op jit(solution)/shard_map/while/body/eval_jaxpr/psum | solution.py:37
  767.2 1.0 copy-start
  958.5 187.4 %all-reduce.2.cloned.1.call-start = ((), (), s32[]{:S(2)}) async-start(), calls=%async_computation.1 | async-start | bytes 2097152 | tf_op jit(solution)/shard_map/while/body/eval_jaxpr/psum | solution.py:37
  958.7 1.0 copy-start
  1150.5 187.7 %all-reduce.2.cloned.1.call-start = ((), (), s32[]{:S(2)}) async-start(), calls=%async_computation.1 | async-start | bytes 2097152 | tf_op jit(solution)/shard_map/while/body/eval_jaxpr/psum | solution.py:37
  1150.7 1.0 copy-start
  1342.9 187.7 %all-reduce.2.cloned.1.call-start = ((), (), s32[]{:S(2)}) async-start(), calls=%async_computation.1 | async-start | bytes 2097152 | tf_op jit(solution)/shard_map/while/body/eval_jaxpr/psum | solution.py:37
  1343.1 1.0 copy-start
  1535.2 187.7 %all-reduce.2.cloned.1.call-start = ((), (), s32[]{:S(2)}) async-start(), calls=%async_computation.1 | async-start | bytes 2097152 | tf_op jit(solution)/shard_map/while/body/eval_jaxpr/psum | solution.py:37
  1535.4 1.0 copy-start
Sparse Core Ops, SparseCore 0:
  9.2 159.5 all-gather.1
  191.6 186.3 all-reduce.1
  386.9 183.4 all-reduce.1
  578.9 183.4 all-reduce.1
  771.0 182.8 all-reduce.1
  962.4 183.4 all-reduce.1
  1154.8 183.3 all-reduce.1
  1347.2 183.4 all-reduce.1
  1539.5 183.4 all-reduce.1
where the time goes:
time: 1740 us; the launch traced here: 1730 us
  waiting for transfers between devices  1650 us (95%)
  matrix products  31.5 us (2%)
  local copies, waits for them, and re-layouts  28.1 us (2%)
    psum x8, waiting for transfers between devices, advance(): panel_solved = lax.psum(term, 'row')  1490 us
    all_gather x1, waiting for transfers between devices, shards(): whole_factor = lax.all_gather(factor, 'col', axis=1, tiled=True)  161 us
  transfers between devices with their start and end apart: 9, of which 9 were waited for; matrix products, arithmetic and copies ran while one was open for 0% of the time, Pallas kernels for 0%

commit v1 on v0

--- a/solution.py
+++ b/solution.py
@@ -2,6 +2,11 @@
 import jax.numpy as jnp
 from jax import lax
 from jax.sharding import PartitionSpec as P
+
+
+def all_by_exchange(value, axis, d):
+    repeated = jnp.stack([value] * lax.axis_size(axis))
+    return jnp.concatenate(lax.all_to_all(repeated, axis, 0, 0), axis=d)
 
 
 def shards(factor, diag_inverse, phenotypes):
@@ -13,7 +18,7 @@
     my_offset = my_row % per_panel * rows_here
     local_blocks = factor.shape[1]
     panel_count = local_blocks * lax.axis_size("col") // per_panel
-    whole_factor = lax.all_gather(factor, "col", axis=1, tiled=True)
+    whole_factor = all_by_exchange(factor, "col", 1)
     flat_factor = whole_factor.reshape(rows_here, -1)
     empty = jnp.zeros(phenotypes.shape, jnp.float32)
 

time: 1740 us -> 1790 us (1.029)
  waiting for transfers between devices: 1650 us -> 1670 us
    all_to_all x0 -> x1, waiting for transfers between devices: none -> 181 us  [all_by_exchange(): return jnp.concatenate(lax.all_to_all(repeated, axis, 0, 0), axis=d)]
    all_gather x1 -> x0, waiting for transfers between devices: 161 us -> none  [shards(): whole_factor = lax.all_gather(factor, 'col', axis=1, tiled=True)]
    all_to_all x0 -> x1, local copies, waits for them, and re-layouts: none -> 19.2 us  [all_by_exchange(): return jnp.concatenate(lax.all_to_all(repeated, axis, 0, 0), axis=d)]
    unnamed x3 -> x2, local copies, waits for them, and re-layouts: 18.6 us -> 0.01 us
where the time goes in v1:
time: 1790 us
  waiting for transfers between devices  1670 us (93%)
  matrix products  44.5 us (2%)
  local copies, waits for them, and re-layouts  39.3 us (2%)
    psum x8, waiting for transfers between devices, advance(): panel_solved = lax.psum(term, 'row')  1490 us
    all_to_all x1, waiting for transfers between devices, all_by_exchange(): return jnp.concatenate(lax.all_to_all(repeated, axis, 0, 0), axis=d)  181 us
    dot_general x8, matrix products, advance(): jnp.dot(columns, panel_solved, precision=lax.Precision.HIGHEST, preferred...  42.4 us
  transfers between devices with their start and end apart: 9, of which 9 were waited for; matrix products, arithmetic and copies ran while one was open for 0% of the time, Pallas kernels for 0%

profile of v1, /device:TPU:2, one launch (start us, length us, event | category | flops | bytes accessed | tf_op | source)
XLA Modules:
  0.0 1788.3 jit_solution(10567511947867886816)
XLA Ops:
  6.5 10.5 stack.2
  17.0 9.2 all-to-all-start
  26.2 180.6 %all-to-all-done = f32[4,256,16,256]{3,2,1,0:T(8,128)} async-done(((f32[4,256,16,256]{3,2,1,0:T(8,128)}), f32[4,256,16,256]{3,2,1,0:T(8,128)}, u32[]{:S(2)}, u32[]{:S(2)}) %all-to-all-start) | async-done | bytes 16777248 | tf_op jit(solution)/shard_map/all_to_all | solution.py:9
  206.8 19.2 %copy.6 = f32[4,256,16,256]{1,3,2,0:T(8,128)} copy(f32[4,256,16,256]{3,2,1,0:T(8,128)} %all-to-all-done) | data formatting | bytes 33554432 | tf_op jit(solution)/shard_map/all_to_all | solution.py:9
  226.1 1554.6 %while.18 = (s32[]{:T(128)}, f32[256,128]{1,0:T(8,128)S(1)}, f32[256,128]{0,1:T(8,128)S(1)}, f32[256,16384]{0,1:T(8,128)}, s32[]{:T(128)}, /*index=5*/f32[256,12...) while((s32[]{:T(128)}, f32[256,128]{1,0:T(8,128)S(1)}, ...), condition=%wide.region_4.5_spmd.clone, body=%wide.region_0.4_spmd.clone.sunk | while | flops 1611038720 | bytes 17957160 | solution.py:53
  226.1 2.2 conditional.3
  226.1 2.1 convolution_bitcast_fusion
  228.3 1.0 copy-done
  229.3 0.0 all-reduce.2.cloned.1.call-update
  229.3 188.4 %all-reduce.2.cloned.1.call-done = f32[2048,128]{0,1:T(8,128)} async-done(((f32[2048,128]{0,1:T(8,128)}), f32[2048,128]{0,1:T(8,128)}) %all-reduce.2.cloned.1.call-update) | async-done | bytes 1048592 | tf_op jit(solution)/shard_map/while/body/eval_jaxpr/psum | solution.py:42
  417.7 5.3 fusion.14
  423.0 0.9 select_select_fusion.2
  424.0 0.0 all-reduce.2.cloned.1.call-start
  424.1 0.1 conditional.3
  424.1 0.1 broadcast.6
  424.2 1.0 copy-done
  425.2 186.5 %all-reduce.2.cloned.1.call-done = f32[2048,128]{0,1:T(8,128)} async-done(((f32[2048,128]{0,1:T(8,128)}), f32[2048,128]{0,1:T(8,128)}) %all-reduce.2.cloned.1.call-update) | async-done | bytes 1048592 | tf_op jit(solution)/shard_map/while/body/eval_jaxpr/psum | solution.py:42
  611.7 5.3 fusion.14
  617.0 0.9 select_select_fusion.2
  618.0 0.0 all-reduce.2.cloned.1.call-start
  618.0 0.1 conditional.3
  618.1 0.1 broadcast.6
  618.2 1.0 copy-done
  619.2 0.0 all-reduce.2.cloned.1.call-update
  619.2 186.5 %all-reduce.2.cloned.1.call-done = f32[2048,128]{0,1:T(8,128)} async-done(((f32[2048,128]{0,1:T(8,128)}), f32[2048,128]{0,1:T(8,128)}) %all-reduce.2.cloned.1.call-update) | async-done | bytes 1048592 | tf_op jit(solution)/shard_map/while/body/eval_jaxpr/psum | solution.py:42
  805.7 5.3 fusion.14
  811.0 0.9 select_select_fusion.2
  812.0 0.0 all-reduce.2.cloned.1.call-start
  812.1 0.1 conditional.3
  812.1 0.1 broadcast.6
  812.2 1.0 copy-done
  813.2 186.1 %all-reduce.2.cloned.1.call-done = f32[2048,128]{0,1:T(8,128)} async-done(((f32[2048,128]{0,1:T(8,128)}), f32[2048,128]{0,1:T(8,128)}) %all-reduce.2.cloned.1.call-update) | async-done | bytes 1048592 | tf_op jit(solution)/shard_map/while/body/eval_jaxpr/psum | solution.py:42
  999.4 5.3 fusion.14
  1004.7 0.9 select_select_fusion.2
  1005.6 0.0 all-reduce.2.cloned.1.call-start
  1005.7 0.1 conditional.3
  1005.7 0.1 broadcast.6
  1005.9 1.0 copy-done
  1006.9 0.0 all-reduce.2.cloned.1.call-update
  1006.9 186.2 %all-reduce.2.cloned.1.call-done = f32[2048,128]{0,1:T(8,128)} async-done(((f32[2048,128]{0,1:T(8,128)}), f32[2048,128]{0,1:T(8,128)}) %all-reduce.2.cloned.1.call-update) | async-done | bytes 1048592 | tf_op jit(solution)/shard_map/while/body/eval_jaxpr/psum | solution.py:42
  1193.1 5.3 fusion.14
  1198.4 0.9 select_select_fusion.2
  1199.3 0.0 all-reduce.2.cloned.1.call-start
  1199.4 0.1 conditional.3
  1199.4 0.1 broadcast.6
  1199.6 1.0 copy-done
  1200.6 185.9 %all-reduce.2.cloned.1.call-done = f32[2048,128]{0,1:T(8,128)} async-done(((f32[2048,128]{0,1:T(8,128)}), f32[2048,128]{0,1:T(8,128)}) %all-reduce.2.cloned.1.call-update) | async-done | bytes 1048592 | tf_op jit(solution)/shard_map/while/body/eval_jaxpr/psum | solution.py:42
  1386.5 5.3 fusion.14
  1391.8 0.9 select_select_fusion.2
  1392.7 0.0 all-reduce.2.cloned.1.call-start
  1392.8 0.1 conditional.3
  1392.8 0.1 broadcast.6
  1392.9 1.0 copy-done
  1394.0 186.5 %all-reduce.2.cloned.1.call-done = f32[2048,128]{0,1:T(8,128)} async-done(((f32[2048,128]{0,1:T(8,128)}), f32[2048,128]{0,1:T(8,128)}) %all-reduce.2.cloned.1.call-update) | async-done | bytes 1048592 | tf_op jit(solution)/shard_map/while/body/eval_jaxpr/psum | solution.py:42
  1580.4 5.3 fusion.14
  1585.7 0.9 select_select_fusion.2
  1586.7 0.0 all-reduce.2.cloned.1.call-start
  1586.8 0.1 conditional.3
  1586.8 0.1 broadcast.6
  1586.9 1.0 copy-done
  1588.0 186.5 %all-reduce.2.cloned.1.call-done = f32[2048,128]{0,1:T(8,128)} async-done(((f32[2048,128]{0,1:T(8,128)}), f32[2048,128]{0,1:T(8,128)}) %all-reduce.2.cloned.1.call-update) | async-done | bytes 1048592 | tf_op jit(solution)/shard_map/while/body/eval_jaxpr/psum | solution.py:42
  1774.5 5.3 fusion.14
  1779.8 0.9 select_select_fusion.2
  1780.7 0.8 copy.8
  (26 shorter events, 0.2 us)
Async XLA Ops:
  17.0 189.8 %all-to-all-start = ((f32[4,256,16,256]{3,2,1,0:T(8,128)}), f32[4,256,16,256]{3,2,1,0:T(8,128)}, u32[]{:S(2)}, u32[]{:S(2)}) async-start(f32[4,256,16,256]{3,2,1,0:T(8,128)} %stack.2), calls=%async_computation | async-start | bytes 33554432 | tf_op jit(solution)/shard_map/all_to_all | solution.py:9
  26.2 199.9 %copy-start.1 = (f32[256,2048]{1,0:T(8,128)S(1)}, f32[256,2048]{1,0:T(8,128)}, u32[]{:S(2)}) copy-start(f32[256,2048]{1,0:T(8,128)} %param.8) | copy-start | bytes 6291460
  226.1 191.7 %all-reduce.2.cloned.1.call-start = ((), (), s32[]{:S(2)}) async-start(), calls=%async_computation.1 | async-start | bytes 2097152 | tf_op jit(solution)/shard_map/while/body/eval_jaxpr/psum | solution.py:42
  228.3 1.0 copy-start
  424.0 187.7 %all-reduce.2.cloned.1.call-start = ((), (), s32[]{:S(2)}) async-start(), calls=%async_computation.1 | async-start | bytes 2097152 | tf_op jit(solution)/shard_map/while/body/eval_jaxpr/psum | solution.py:42
  424.2 1.0 copy-start
  618.0 187.7 %all-reduce.2.cloned.1.call-start = ((), (), s32[]{:S(2)}) async-start(), calls=%async_computation.1 | async-start | bytes 2097152 | tf_op jit(solution)/shard_map/while/body/eval_jaxpr/psum | solution.py:42
  618.2 1.0 copy-start
  812.0 187.4 %all-reduce.2.cloned.1.call-start = ((), (), s32[]{:S(2)}) async-start(), calls=%async_computation.1 | async-start | bytes 2097152 | tf_op jit(solution)/shard_map/while/body/eval_jaxpr/psum | solution.py:42
  812.2 1.0 copy-start
  1005.6 187.4 %all-reduce.2.cloned.1.call-start = ((), (), s32[]{:S(2)}) async-start(), calls=%async_computation.1 | async-start | bytes 2097152 | tf_op jit(solution)/shard_map/while/body/eval_jaxpr/psum | solution.py:42
  1005.8 1.0 copy-start
  1199.3 187.1 %all-reduce.2.cloned.1.call-start = ((), (), s32[]{:S(2)}) async-start(), calls=%async_computation.1 | async-start | bytes 2097152 | tf_op jit(solution)/shard_map/while/body/eval_jaxpr/psum | solution.py:42
  1199.5 1.0 copy-start
  1392.7 187.7 %all-reduce.2.cloned.1.call-start = ((), (), s32[]{:S(2)}) async-start(), calls=%async_computation.1 | async-start | bytes 2097152 | tf_op jit(solution)/shard_map/while/body/eval_jaxpr/psum | solution.py:42
  1392.9 1.0 copy-start
  1586.7 187.7 %all-reduce.2.cloned.1.call-start = ((), (), s32[]{:S(2)}) async-start(), calls=%async_computation.1 | async-start | bytes 2097152 | tf_op jit(solution)/shard_map/while/body/eval_jaxpr/psum | solution.py:42
  1586.9 1.0 copy-start
Sparse Core Ops, SparseCore 0:
  230.3 187.3 all-reduce.1
  428.2 183.4 all-reduce.1
  622.2 183.4 all-reduce.1
  815.9 183.4 all-reduce.1
  1009.6 183.4 all-reduce.1
  1203.3 183.1 all-reduce.1
  1397.0 183.4 all-reduce.1
  1591.0 183.4 all-reduce.1
